TPU v7x, 512 devices: a whole 4x4x16 slice. The times are simulated.
512 devices in a mesh: ha: 4 (over x), wa: 16 (over y, z_hi, core), ta: 8 (over z_lo).
Axes of the slice: x: 4, y: 4, z: 16 (z_hi: 2, z_lo: 8; z = z_hi * 8 + z_lo), core: 2. Of those that a mesh axis runs over, the one named last changes fastest.
Arguments:
- hidden_states: bfloat16 [2, 96, 128, 5120], P(None, 'ha', 'wa', 'ta'), may hold values from -60 to 60
- queries: bfloat16 [2, 96, 128, 5120], P(None, 'ha', 'wa', 'ta'), may hold values from -120 to 120
- keys_values: bfloat16 [2, 2, 96, 128, 5120], P(None, None, 'ha', 'wa', 'ta'), may hold values from -16 to 16
- out_weight: bfloat16 [5120, 5120], P('ta', 'wa'), may hold values from -0.078125 to 0.078125
- mod_table: float32 [50, 3, 5120], P(None, None, 'ta'), may hold values from -4 to 4
- windows: int32 [40, 2], P('ta'), may hold values from 0 to 1, as said below
- step_index: int32 [1], replicated, may hold values from 0 to 49
Outputs:
- residual_out: bfloat16 [2, 96, 128, 5120], P(None, 'ha', 'wa', 'ta')
- ffn_input: bfloat16 [2, 96, 128, 5120], P(None, 'ha', 'wa', 'ta')
Inputs may be any that keep to these rules, and one draw needn't show every extreme that they name: `windows`: some head has both radii equal to 1.
All inputs are finite; a program needn't handle non-finite values.
Results may differ from a plain program's by a relative error of at most 0.0085.
Values may be sent and summed in bfloat16 or wider, within the bound.
A program may use at most 64 MiB of HBM per device.

v0:
```python
from functools import partial
from functools import reduce
import math

import jax
import jax.numpy as jnp
from jax import lax
from jax.sharding import PartitionSpec as P

D = 5120
HD = 128
TILE = 8


EPSILON = 1e-06


def padded_2(block, sides, width):
    for axis, dim in sides:
        count = lax.axis_size(axis)
        forward = [(i, i + 1) for i in range(count - 1)]
        backward = [(target, source) for source, target in forward]
        low = lax.ppermute(
            lax.slice_in_dim(block, block.shape[dim] - width, None, axis=dim), axis, forward
        )
        high = lax.ppermute(lax.slice_in_dim(block, 0, width, axis=dim), axis, backward)
        block = jnp.concatenate([low, block, high], axis=dim)
    return block


def key_set(block, first_row, first_col, placing):
    row_base, col_base, rows_total, cols_total, query_trow, query_tcol = placing
    grid_shape = (block.shape[1], block.shape[2], block.shape[3])
    global_row = row_base + (first_row - TILE) + lax.broadcasted_iota(jnp.int32, grid_shape, 1)
    global_col = col_base + (first_col - TILE) + lax.broadcasted_iota(jnp.int32, grid_shape, 2)
    inside = (
        (global_row >= 0)
        & (global_row < rows_total)
        & (global_col >= 0)
        & (global_col < cols_total)
    ).reshape(-1)
    row_gap = jnp.abs(jnp.floor_divide(global_row, TILE).reshape(-1)[None, :] - query_trow[:, None])
    col_gap = jnp.abs(jnp.floor_divide(global_col, TILE).reshape(-1)[None, :] - query_tcol[:, None])
    entries = grid_shape[0] * grid_shape[1] * grid_shape[2]
    feature_count = block.shape[4]
    return (
        block[0].reshape(entries, feature_count),
        block[1].reshape(entries, feature_count),
        row_gap,
        col_gap,
        inside,
    )


def head_output(index, key_sets, query_rows, windows, head_size):
    radius_row = windows[index, 0]
    radius_col = windows[index, 1]
    query_head = lax.dynamic_slice_in_dim(query_rows, index * head_size, head_size, 1)
    scale = 1.0 / math.sqrt(HD)
    masked = []
    value_heads = []
    for keys_all, values_all, row_gap, col_gap, inside in key_sets:
        key_head = lax.dynamic_slice_in_dim(keys_all, index * head_size, head_size, 1)
        value_heads.append(lax.dynamic_slice_in_dim(values_all, index * head_size, head_size, 1))
        raw = (
            lax.dot_general(
                query_head, key_head, (((1,), (1,)), ((), ())), preferred_element_type=jnp.float32
            )
            * scale
        )
        allowed = inside[None, :] & (row_gap <= radius_row) & (col_gap <= radius_col)
        masked.append(jnp.where(allowed, raw, -jnp.inf))
    highest = reduce(jnp.maximum, [jnp.max(scores, axis=1) for scores in masked])
    expos = [jnp.exp(scores - highest[:, None]) for scores in masked]
    total = reduce(jnp.add, [jnp.sum(expo, axis=1) for expo in expos])
    output = reduce(
        jnp.add,
        [
            jnp.dot(
                (expo / total[:, None]).astype(jnp.bfloat16),
                value_head,
                preferred_element_type=jnp.float32,
            )
            for expo, value_head in zip(expos, value_heads)
        ],
    )
    return output.astype(jnp.bfloat16)


def group_sum(terms):
    return lax.psum_scatter(
        terms.astype(jnp.bfloat16), "ta", scatter_dimension=1, tiled=True
    ).astype(jnp.float32)


def shards(hidden_states, queries, keys_values, out_weight, mod_table, windows, step_index):
    frame_count, row_count, col_count, feature_count = queries.shape
    head_count = windows.shape[0]
    head_size = feature_count // head_count
    token_count = frame_count * row_count * col_count
    row_base = lax.axis_index("ha") * row_count
    col_base = lax.axis_index("wa") * col_count
    rows_total = row_count * lax.axis_size("ha")
    cols_total = col_count * lax.axis_size("wa")
    grid_shape = (frame_count, row_count, col_count)
    query_trow = jnp.floor_divide(
        row_base + lax.broadcasted_iota(jnp.int32, grid_shape, 1), TILE
    ).reshape(-1)
    query_tcol = jnp.floor_divide(
        col_base + lax.broadcasted_iota(jnp.int32, grid_shape, 2), TILE
    ).reshape(-1)
    placing = (row_base, col_base, rows_total, cols_total, query_trow, query_tcol)
    query_rows = queries.reshape(token_count, feature_count)
    padded = padded_2(keys_values, (("ha", 2), ("wa", 3)), TILE)
    key_sets = [key_set(padded, 0, 0, placing)]
    heads_out = lax.map(
        partial(
            head_output,
            key_sets=key_sets,
            query_rows=query_rows,
            windows=windows,
            head_size=head_size,
        ),
        jnp.arange(head_count, dtype=jnp.int32),
    )
    piece = lax.all_gather(out_weight, "wa", axis=1, tiled=True)
    terms = jnp.einsum(
        "htd,hdc->tc",
        heads_out,
        piece.reshape(head_count, head_size, piece.shape[1]),
        preferred_element_type=jnp.float32,
    )
    summed = group_sum(terms)
    select = lax.broadcasted_iota(jnp.int32, (mod_table.shape[0], 1, 1), 0) == step_index[0]
    picked = jnp.sum(jnp.where(select, mod_table, 0.0), axis=0)
    local_width = hidden_states.shape[3]
    mixed = hidden_states.reshape(token_count, local_width).astype(jnp.float32) + picked[0] * summed
    sum_first, sum_second = lax.psum((jnp.sum(mixed, axis=1), jnp.sum(mixed * mixed, axis=1)), "ta")
    average = (sum_first / D)[:, None]
    variance = (sum_second / D)[:, None] - average * average
    normed = (mixed - average) * lax.rsqrt(variance + EPSILON)
    ffn_input = (normed * (1.0 + picked[2]) + picked[1]).astype(jnp.bfloat16)
    residual_out = mixed.astype(jnp.bfloat16)
    out_shape = (frame_count, row_count, col_count, local_width)
    return (residual_out.reshape(out_shape), ffn_input.reshape(out_shape))


def solution(mesh):
    return jax.shard_map(
        shards,
        mesh=mesh,
        in_specs=(
            P(None, "ha", "wa", "ta"),
            P(None, "ha", "wa", "ta"),
            P(None, None, "ha", "wa", "ta"),
            P("ta", "wa"),
            P(None, None, "ta"),
            P("ta", None),
            P(),
        ),
        out_specs=(P(None, "ha", "wa", "ta"), P(None, "ha", "wa", "ta")),
        check_vma=False,
    )
```

profile of v0, /device:TPU:2, one launch (start us, length us, event | category | flops | bytes accessed | tf_op | source)
XLA Modules:
  0.0 444.1 jit_solution(17170450920897944213)
XLA Ops:
  7.2 0.7 all-gather.2.cloned.1.call-update
  8.0 1.1 fusion.26
  9.1 3.4 collective-permute-start
  12.5 6.4 %collective-permute-start.1 = (bf16[2,2,8,8,640]{4,3,2,1,0:T(8,128)(2,1)S(1)}, bf16[2,2,8,8,640]{4,3,2,1,0:T(8,128)(2,1)S(1)}, u32[]{:S(2)}, u32[]{:S(2)}) collective-permute-start(bf16[2,2,8,8,640]{4,3,2,1,0:T(8,128)(2,1)S(1)} %get-tuple-element.137), channel_id=1, source_target_pairs={{128,0},{256,128},{384,256},{129,1},{257,129},{385,257},{130,2},{2... | collective-permute-start | bytes 983048 | tf_op jit(solution)/shard_map/ppermute | solution.py:26
  19.0 2.4 collective-permute-done
  21.4 1.0 constant_dynamic-update-slice_fusion.2
  22.6 0.9 collective-permute-done.1
  23.6 2.6 collective-permute-start.2
  26.2 1.3 collective-permute-start.3
  28.2 16.3 %collective-permute-done.3 = bf16[2,2,40,8,640]{4,3,2,1,0:T(8,128)(2,1)} collective-permute-done((bf16[2,2,40,8,640]{4,3,2,1,0:T(8,128)(2,1)S(1)}, bf16[2,2,40,8,640]{4,3,2,1,0:T(8,128)(2,1)}, u32[]{:S(2)}, u32[]{:S(2)}) %collective-permute-start.3) | collective-permute-done | bytes 1638432 | tf_op jit(solution)/shard_map/ppermute | solution.py:26
  44.5 2.1 pad_maximum_fusion
  46.6 1.9 fusion.25
  48.6 48.4 %while.11 = (s32[]{:T(128)}, bf16[5,384,128]{2,1,0:T(8,128)(2,1)S(1)}, s32[5]{0:T(128)S(1)}, s32[5,2]{0,1:T(2,128)S(1)}, bf16[384,640]{1,0:T(8,128)(2,1)}, /*ind...) while((s32[]{:T(128)}, ...), condition=%wide.region_4.5_spmd.clone, body=%wide.region_1.4_spmd.clone.sunk | while | flops 389336064 | bytes 10064253 | solution.py:116
  52.6 4.4 fusion.34
  57.5 0.7 fusion.36
  62.3 4.4 fusion.34
  67.2 0.7 fusion.36
  71.1 0.7 constant_dynamic-slice_fusion.3
  72.0 4.4 fusion.34
  76.9 0.7 fusion.36
  81.6 4.4 fusion.34
  86.6 0.7 fusion.36
  91.3 4.4 fusion.34
  96.2 0.7 fusion.36
  97.0 188.2 %all-gather.2.cloned.1.call-done = bf16[640,5120]{0,1:T(8,128)(2,1)} async-done(((bf16[640,320]{0,1:T(8,128)(2,1)}), bf16[640,5120]{0,1:T(8,128)(2,1)}) %all-gather.2.cloned.1.call-update) | async-done | bytes 6553616 | tf_op jit(solution)/shard_map/all_gather | solution.py:126
  285.1 9.6 %copy.11 = bf16[640,5120]{1,0:T(8,128)(2,1)} copy(bf16[640,5120]{0,1:T(8,128)(2,1)} %all-gather.2.cloned.1.call-done) | data formatting | bytes 13107200 | tf_op jit(solution)/shard_map/all_gather | solution.py:126
  294.7 7.6 %bitcast_convert_fusion = bf16[384,5120]{1,0:T(8,128)(2,1)} fusion(bf16[5,384,128]{2,1,0:T(8,128)(2,1)S(1)} %get-tuple-element.54, bf16[5,128,5120]{2,1,0:T(8,128)(2,1)} %bitcast.36), kind=kOutput, calls=%fused_computation.24 | convolution fusion | flops 2518548480 | bytes 10977280 | tf_op jit(solution)/shard_map/htd,hdc->tc/dot_general | solution.py:127
  302.3 6.3 %copy.12 = bf16[384,5120]{0,1:T(8,128)(2,1)} copy(bf16[384,5120]{1,0:T(8,128)(2,1)} %bitcast_convert_fusion) | data formatting | bytes 7864320
  309.7 98.1 %reduce-scatter.4.cloned.1.call-done = bf16[640,384]{1,0:T(8,128)(2,1)} async-done(((bf16[5120,384]{1,0:T(8,128)(2,1)}), bf16[640,384]{1,0:T(8,128)(2,1)}) %reduce-scatter.4.cloned.1.call-update) | async-done | bytes 491536
  407.9 1.3 copy.13
  409.5 26.5 %all-reduce = (f32[384]{0:T(512)S(1)}, f32[384]{0:T(512)S(1)}) all-reduce(f32[384]{0:T(512)S(1)} %get-tuple-element.95, f32[384]{0:T(512)S(1)} %get-tuple-element.94), channel_id=1, replica_groups=mesh['ha'=4,'wa'=16,'ta'=8] {'ta'}, use_global_device_ids=true, to_apply=%region_9.10 | all-reduce | flops 768 | bytes 6144 | tf_op jit(solution)/shard_map/psum | solution.py:138
  436.0 1.3 add_convert_fusion
  (64 shorter events, 10.9 us)
Async XLA Ops:
  7.2 15.3 %copy-start = (bf16[2,2,24,8,640]{4,3,2,1,0:T(8,128)(2,1)S(1)}, bf16[2,2,24,8,640]{4,3,2,1,0:T(8,128)(2,1)}, u32[]{:S(2)}) copy-start(bf16[2,2,24,8,640]{4,3,2,1,0:T(8,128)(2,1)} %param.11) | copy-start | bytes 2949124
  7.2 278.0 %all-gather.2.cloned.1.call-start = ((), (), s32[]{:S(2)}) async-start(), calls=%async_computation.1 | async-start | bytes 6963200 | tf_op jit(solution)/shard_map/all_gather | solution.py:126
  7.9 399.9 %reduce-scatter.4.cloned.1.call-start = ((), (), s32[]{:S(2)}) async-start(), calls=%async_computation.2 | async-start | bytes 4423680
  9.1 12.3 %collective-permute-start = (bf16[2,2,8,8,640]{4,3,2,1,0:T(8,128)(2,1)S(1)}, bf16[2,2,8,8,640]{4,3,2,1,0:T(8,128)(2,1)}, u32[]{:S(2)}, u32[]{:S(2)}) collective-permute-start(bf16[2,2,8,8,640]{4,3,2,1,0:T(8,128)(2,1)S(1)} %get-tuple-element.138), channel_id=1, source_target_pairs={{0,128},{128,256},{256,384},{1,129},{129,257},{257,385},{2,130},{1... | collective-permute-start | bytes 983048 | tf_op jit(solution)/shard_map/ppermute | solution.py:23
  12.5 11.1 %collective-permute-start.1 = (bf16[2,2,8,8,640]{4,3,2,1,0:T(8,128)(2,1)S(1)}, bf16[2,2,8,8,640]{4,3,2,1,0:T(8,128)(2,1)S(1)}, u32[]{:S(2)}, u32[]{:S(2)}) collective-permute-start(bf16[2,2,8,8,640]{4,3,2,1,0:T(8,128)(2,1)S(1)} %get-tuple-element.137), channel_id=1, source_target_pairs={{128,0},{256,128},{384,256},{129,1},{257,129},{385,257},{130,2},{2... | collective-permute-start | bytes 983048 | tf_op jit(solution)/shard_map/ppermute | solution.py:26
  23.6 4.5 %collective-permute-start.2 = (bf16[2,2,40,8,640]{4,3,2,1,0:T(8,128)(2,1)S(1)}, bf16[2,2,40,8,640]{4,3,2,1,0:T(8,128)(2,1)}, u32[]{:S(2)}, u32[]{:S(2)}) collective-permute-start(bf16[2,2,40,8,640]{4,3,2,1,0:T(8,128)(2,1)S(1)} %constant_dynamic-update-slice_fusion), channel_id=1, source_target_pairs={{0,8},{8,16},{16,24},{24,32},{32,40},{40,48},{48,56},{56,64},{64,7... | collective-permute-start | bytes 4915208 | tf_op jit(solution)/shard_map/ppermute | solution.py:23
  26.2 18.3 %collective-permute-start.3 = (bf16[2,2,40,8,640]{4,3,2,1,0:T(8,128)(2,1)S(1)}, bf16[2,2,40,8,640]{4,3,2,1,0:T(8,128)(2,1)}, u32[]{:S(2)}, u32[]{:S(2)}) collective-permute-start(bf16[2,2,40,8,640]{4,3,2,1,0:T(8,128)(2,1)S(1)} %constant_dynamic-update-slice_fusion), channel_id=1, source_target_pairs={{8,0},{16,8},{24,16},{32,24},{40,32},{48,40},{56,48},{64,56},{72,6... | collective-permute-start | bytes 4915208 | tf_op jit(solution)/shard_map/ppermute | solution.py:26
  46.6 2.0 copy-start.3
  46.6 2.0 copy-start.4
  308.5 1.0 copy-start.2
  308.6 100.6 %copy-start.1 = (bf16[2,24,8,640]{3,2,1,0:T(8,128)(2,1)S(1)}, bf16[2,24,8,640]{3,2,1,0:T(8,128)(2,1)}, u32[]{:S(2)}) copy-start(bf16[2,24,8,640]{3,2,1,0:T(8,128)(2,1)} %param.9) | copy-start | bytes 1474564
Sparse Core Ops, SparseCore 0:
  11.3 273.8 all-gather.1
  308.7 99.1 reduce-scatter.3
where the time goes:
time: 445 us; the launch traced here: 444 us
  waiting for transfers between devices  307 us (69%)
  matrix products  32.9 us (7%)
  local copies, waits for them, and re-layouts  28.8 us (6%)
  blocking collectives  26.5 us (6%)
  between operations  15 us (3%)
  starting transfers between devices  13.8 us (3%)
  loops' own time  13.1 us (3%)
  other arithmetic  7.26 us (2%)
    all_gather x1, waiting for transfers between devices, shards(): piece = lax.all_gather(out_weight, 'wa', axis=1, tiled=True)  188 us
    unnamed x3, waiting for transfers between devices  98.8 us
    psum x1, blocking collectives, shards(): lax.psum((jnp.sum(mixed, axis=1), jnp.sum(mixed * mixed, axis=1)), 'ta')  26.5 us
    dot_general x5, matrix products, head_output(): lax.dot_general(query_head, key_head, (((1,), (1,)), ((), ())), preferred...  21.8 us
    ppermute x2, waiting for transfers between devices, padded_2(): lax.ppermute(lax.slice_in_dim(block, 0, width, axis=dim), axis, backward)  17.3 us
    another operation x1, loops' own time, shards(): lax.map(partial(head_output, key_sets=key_sets, query_rows=query_rows, wi...  13.1 us
    all_gather x1, local copies, waits for them, and re-layouts, shards(): piece = lax.all_gather(out_weight, 'wa', axis=1, tiled=True)  9.59 us
    unnamed x14, local copies, waits for them, and re-layouts  8.98 us
  transfers between devices with their start and end apart: 6, of which 5 were waited for; matrix products, arithmetic and copies ran while one was open for 10% of the time, Pallas kernels for 0%

commit v1 on v0

v1 whole, which is shorter than its diff:
```python
import math

import jax
import jax.numpy as jnp
from jax import lax
from jax.experimental import pallas as pl
from jax.experimental.pallas import tpu as pltpu
from jax.sharding import PartitionSpec as P

D = 5120
HD = 128
TILE = 8
EPSILON = 1e-06

N_HA, N_WA, N_TA = 4, 16, 8
N_Y = 4
FRAMES, ROWS, COLS = 2, 24, 8
FEAT = 640
HEADS_HERE = 5
T_ROWS = ROWS // TILE
TOK = FRAMES * TILE * TILE
HALF = TILE * TILE
TOKENS = T_ROWS * TOK
SHARD = D // N_WA
QUARTER = SHARD // N_HA
N_PIECE = N_TA * T_ROWS
MASKED = -1e30
MESH = pl.DeviceIdType.MESH
NT = (((1,), (1,)), ((), ()))


def kernel(
    win_ref,
    step_ref,
    hid_ref,
    q_ref,
    kv_ref,
    wt_ref,
    mod_ref,
    res_ref,
    ffn_ref,
    own,
    par,
    far,
    wall,
    hid,
    qry,
    mod,
    att,
    o_part,
    m_part,
    l_part,
    slot_r,
    slot_l,
    mixed,
    stat,
    lsem,
    ssem,
    rsem,
    ssem_r,
    rsem_r,
    ssem_l,
    rsem_l,
    ssem_s,
    rsem_s,
):
    x = lax.axis_index("ha")
    wa = lax.axis_index("wa")
    g = lax.axis_index("ta")
    y = wa // 4
    zh = lax.rem(wa // 2, 2)
    c = lax.rem(wa, 2)
    nw = 4 * y + 2 * (1 - zh) + c

    dev_par = (x, 4 * y + 2 * zh + 1 - c, g)
    dev_far = (x, lax.rem(wa + 15 + 2 * c, 16), g)
    dev_z = (x, nw, g)
    dev_x = [(lax.rem(x + j + 1, N_HA), wa, g) for j in range(3)]
    dev_y = [(x, lax.rem(wa + 4 * (j + 1), 16), g) for j in range(3)]
    dev_t = [(x, wa, lax.rem(g + j + 1, N_TA)) for j in range(7)]

    def shard_rows(index):
        return pl.ds(pl.multiple_of(index * SHARD, SHARD), SHARD)

    def quarter_rows(index, part):
        return pl.ds(pl.multiple_of(index * SHARD + part * QUARTER, QUARTER), QUARTER)

    loads = []
    for f in range(FRAMES):
        for r in range(T_ROWS):
            loads.append(
                pltpu.make_async_copy(
                    kv_ref.at[:, f, pl.ds(r * HALF, HALF), :],
                    own.at[:, pl.ds((r + 1) * TOK + f * HALF, HALF), :],
                    lsem.at[f * T_ROWS + r],
                )
            )
    load_w = pltpu.make_async_copy(wt_ref, wall.at[shard_rows(wa)], lsem.at[6])
    load_q = pltpu.make_async_copy(q_ref, qry, lsem.at[7])
    load_h = pltpu.make_async_copy(hid_ref, hid, lsem.at[8])
    load_m = pltpu.make_async_copy(mod_ref, mod, lsem.at[9])
    for load in loads:
        load.start()
    load_w.start()
    load_q.start()
    load_h.start()
    load_m.start()

    @pl.when(g == 0)
    def _():
        slot_r[...] = jnp.zeros_like(slot_r)

    @pl.when(g == N_TA - 1)
    def _():
        slot_l[...] = jnp.zeros_like(slot_l)

    barrier = pltpu.get_barrier_semaphore()
    peers = [dev_par, dev_far, dev_z] + dev_x + dev_y + dev_t
    for peer in peers:
        pl.semaphore_signal(barrier, inc=1, device_id=peer, device_id_type=MESH)
    for load in loads:
        load.wait()
    load_w.wait()
    pl.semaphore_wait(barrier, len(peers))

    def remote(index, src, dst, device):
        return pltpu.make_async_remote_copy(
            src_ref=src,
            dst_ref=dst,
            send_sem=ssem.at[index],
            recv_sem=rsem.at[index],
            device_id=device,
            device_id_type=MESH,
        )

    def rows(buf, first, count):
        return buf.at[:, pl.ds(first * TOK, count * TOK), :]

    w_z = remote(0, wall.at[quarter_rows(wa, x)], wall.at[quarter_rows(wa, x)], dev_z)
    far_a = remote(1, rows(own, 1, 1), rows(far, 1, 1), dev_far)
    far_b = remote(2, rows(own, 3, 1), rows(far, 3, 1), dev_far)
    far_c = remote(3, rows(own, 2, 1), rows(far, 2, 1), dev_far)
    up = remote(4, rows(own, 1, 1), rows(own, 4, 1), dev_x[2])
    down = remote(5, rows(own, 3, 1), rows(own, 0, 1), dev_x[0])
    par_mid = remote(6, rows(own, 1, 3), rows(par, 1, 3), dev_par)
    par_top = remote(7, rows(own, 0, 1), rows(par, 0, 1), dev_par)
    par_bot = remote(8, rows(own, 4, 1), rows(par, 4, 1), dev_par)
    far_up = remote(9, rows(far, 1, 1), rows(far, 4, 1), dev_x[2])
    far_down = remote(10, rows(far, 3, 1), rows(far, 0, 1), dev_x[0])
    w_x = [
        remote(11 + j, wall.at[quarter_rows(nw, x)], wall.at[quarter_rows(nw, x)], dev_x[j])
        for j in range(3)
    ]
    w_yn = [
        remote(14 + j, wall.at[shard_rows(wa)], wall.at[shard_rows(wa)], dev_y[j]) for j in range(3)
    ]
    w_yf = [
        remote(17 + j, wall.at[shard_rows(nw)], wall.at[shard_rows(nw)], dev_y[j]) for j in range(3)
    ]
    w_c = [
        remote(20, wall.at[shard_rows(wa)], wall.at[shard_rows(wa)], dev_par),
        remote(21, wall.at[shard_rows(nw)], wall.at[shard_rows(nw)], dev_par),
    ]
    for j in range(3):
        near = lax.rem(wa + 4 * (3 - j), 16)
        w_c.append(remote(22 + j, wall.at[shard_rows(near)], wall.at[shard_rows(near)], dev_par))
    for j in range(3):
        other = lax.rem(nw + 4 * (3 - j), 16)
        w_c.append(remote(25 + j, wall.at[shard_rows(other)], wall.at[shard_rows(other)], dev_par))

    w_z.start()
    far_a.start()
    far_b.start()
    up.start()
    down.start()
    par_mid.start()
    w_c[0].start()
    for copy in w_yn:
        copy.start()

    w_z.wait_recv()
    for copy in w_x:
        copy.start()
    up.wait_recv()
    par_bot.start()
    down.wait_recv()
    par_top.start()
    for copy in w_x:
        copy.wait_recv()
    w_c[1].start()
    for copy in w_yf:
        copy.start()

    par_mid.wait_recv()
    par_top.wait_recv()
    par_bot.wait_recv()
    load_q.wait()
    scale = 1.0 / math.sqrt(HD)
    far_there = jnp.where(c == 0, wa > 0, wa < N_WA - 1)

    def biases(r, head, beside, there):
        radius_row = win_ref[head, 0]
        radius_col = win_ref[head, 1]
        out = []
        for gap in (-1, 0, 1):
            row = T_ROWS * x + r + gap
            ok = (row >= 0) & (row < N_HA * T_ROWS) & (abs(gap) <= radius_row)
            if beside:
                ok = ok & (radius_col >= 1) & there
            out.append(jnp.where(ok, 0.0, MASKED).astype(jnp.float32))
        return out

    def lanes(head):
        return pl.ds(pl.multiple_of(head * HD, HD), HD)

    def token_rows(r, count):
        return pl.ds(pl.multiple_of(r * TOK, TOK), count * TOK)

    def query_tile(r, head):
        part = pl.ds(pl.multiple_of(r * HALF, HALF), HALF)
        return jnp.concatenate([qry[0, part, lanes(head)], qry[1, part, lanes(head)]], axis=0)

    def scores(query, buf, r, head, bias):
        keys = buf[0, token_rows(r, 3), lanes(head)]
        raw = lax.dot_general(query, keys, NT, preferred_element_type=jnp.float32) * scale
        return [raw[:, j * TOK : (j + 1) * TOK] + bias[j] for j in range(3)]

    def values(weights, buf, r, head):
        return jnp.dot(
            jnp.concatenate(weights, axis=1).astype(jnp.bfloat16),
            buf[1, token_rows(r, 3), lanes(head)],
            preferred_element_type=jnp.float32,
        )

    def total(parts, op):
        out = parts[0]
        for part in parts[1:]:
            out = op(out, part)
        return out

    def near_tile(index, carry):
        r = index // HEADS_HERE
        head = lax.rem(index, HEADS_HERE)
        query = query_tile(r, head)
        s_own = scores(query, own, r, head, biases(r, head, False, True))
        s_par = scores(query, par, r, head, biases(r, head, True, True))
        highest = jnp.max(total(s_own + s_par, jnp.maximum), axis=1, keepdims=True)
        p_own = [jnp.exp(s - highest) for s in s_own]
        p_par = [jnp.exp(s - highest) for s in s_par]
        norm = jnp.sum(total(p_own + p_par, jnp.add), axis=1, keepdims=True)
        o_part[index] = values(p_own, own, r, head) + values(p_par, par, r, head)
        m_part[index] = jnp.broadcast_to(highest, (TOK, HD))
        l_part[index] = jnp.broadcast_to(norm, (TOK, HD))
        return carry

    lax.fori_loop(0, T_ROWS * HEADS_HERE, near_tile, 0)

    far_a.wait_send()
    far_c.start()
    far_a.wait_recv()
    far_up.start()
    for j in range(3):
        w_yn[j].wait_recv()
        w_c[2 + j].start()
    far_b.wait_recv()
    far_down.start()
    for j in range(3):
        w_yf[j].wait_recv()
        w_c[5 + j].start()
    far_up.wait_recv()
    far_down.wait_recv()
    far_c.wait_recv()

    def far_tile(index, carry):
        r = index // HEADS_HERE
        head = lax.rem(index, HEADS_HERE)
        query = query_tile(r, head)
        s_far = scores(query, far, r, head, biases(r, head, True, far_there))
        before = m_part[index]
        highest = jnp.maximum(
            before, jnp.max(total(s_far, jnp.maximum), axis=1, keepdims=True)
        )
        shrink = jnp.exp(before - highest)
        p_far = [jnp.exp(s - highest) for s in s_far]
        norm = shrink * l_part[index] + jnp.sum(total(p_far, jnp.add), axis=1, keepdims=True)
        out = (shrink * o_part[index] + values(p_far, far, r, head)) / norm
        att[token_rows(r, 1), lanes(head)] = out.astype(jnp.bfloat16)
        return carry

    lax.fori_loop(0, T_ROWS * HEADS_HERE, far_tile, 0)
    for copy in w_c:
        copy.wait_recv()

    right = (x, wa, lax.rem(g + 1, N_TA))
    left = (x, wa, lax.rem(g + N_TA - 1, N_TA))

    def partial_sum(dest, r):
        weight = wall[pl.ds(pl.multiple_of(dest * FEAT, FEAT), FEAT), :]
        return lax.dot_general(
            att[token_rows(r, 1), :], weight, NT, preferred_element_type=jnp.float32
        )

    def hop_r(k):
        return pltpu.make_async_remote_copy(
            src_ref=slot_r.at[k],
            dst_ref=slot_r.at[k],
            send_sem=ssem_r.at[k],
            recv_sem=rsem_r.at[k],
            device_id=right,
            device_id_type=MESH,
        )

    def hop_l(k):
        return pltpu.make_async_remote_copy(
            src_ref=slot_l.at[k],
            dst_ref=slot_l.at[k],
            send_sem=ssem_l.at[k],
            recv_sem=rsem_l.at[k],
            device_id=left,
            device_id_type=MESH,
        )

    def hop(tau, carry):
        k = tau - 2 * g

        @pl.when((k >= 0) & (k < T_ROWS * (N_TA - 1 - g)))
        def _():
            @pl.when(g > 0)
            def _():
                hop_r(k).wait_recv()

            add = partial_sum(N_TA - 1 - k // T_ROWS, lax.rem(k, T_ROWS))
            slot_r[k] = (slot_r[k].astype(jnp.float32) + add).astype(jnp.bfloat16)
            hop_r(k).start()

        n = tau - 2 * (N_TA - 1 - g)

        @pl.when((n >= 0) & (n < T_ROWS * g))
        def _():
            @pl.when(g < N_TA - 1)
            def _():
                hop_l(n).wait_recv()

            add = partial_sum(n // T_ROWS, lax.rem(n, T_ROWS))
            slot_l[n] = (slot_l[n].astype(jnp.float32) + add).astype(jnp.bfloat16)
            hop_l(n).start()

        return carry

    lax.fori_loop(0, T_ROWS * (N_TA - 1), hop, 0)

    load_h.wait()
    load_m.wait()
    picked = mod[step_ref[0]]
    gate, shift, gain = picked[0:1], picked[1:2], picked[2:3]
    lane = lax.broadcasted_iota(jnp.int32, (TOK, HD), 1)
    for r in range(T_ROWS):
        own_part = partial_sum(g, r)
        k = T_ROWS * (N_TA - 1 - g) + r
        n = T_ROWS * g + r

        @pl.when(g > 0)
        def _():
            hop_r(k).wait_recv()

        @pl.when(g < N_TA - 1)
        def _():
            hop_l(n).wait_recv()

        projected = own_part + slot_r[k].astype(jnp.float32) + slot_l[n].astype(jnp.float32)
        part = pl.ds(r * HALF, HALF)
        before = jnp.concatenate([hid[0, part, :], hid[1, part, :]], axis=0).astype(jnp.float32)
        now = before + gate * projected
        mixed[pl.ds(r * TOK, TOK), :] = now
        rounded = now.astype(jnp.bfloat16)
        res_ref[0, part, :] = rounded[:HALF]
        res_ref[1, part, :] = rounded[HALF:]
        first = jnp.sum(now, axis=1, keepdims=True)
        second = jnp.sum(now * now, axis=1, keepdims=True)
        both = jnp.where(lane == 0, first, jnp.where(lane == 1, second, 0.0))
        stat[0, :, pl.ds(r * TOK, TOK)] = jnp.transpose(both)[:8]

    def share(j):
        return pltpu.make_async_remote_copy(
            src_ref=stat.at[0],
            dst_ref=stat.at[j + 1],
            send_sem=ssem_s.at[j],
            recv_sem=rsem_s.at[j],
            device_id=dev_t[j],
            device_id_type=MESH,
        )

    for j in range(7):
        share(j).start()
    for j in range(7):
        share(j).wait_recv()
    sums = total([stat[j] for j in range(N_TA)], jnp.add)
    for r in range(T_ROWS):
        line = sums[:, r * TOK : (r + 1) * TOK]
        column = jnp.transpose(jnp.concatenate([line] * (HD // 8), axis=0))
        average = column[:, 0:1] / D
        variance = column[:, 1:2] / D - average * average
        now = mixed[pl.ds(r * TOK, TOK), :]
        normed = (now - average) * lax.rsqrt(variance + EPSILON)
        out = (normed * (1.0 + gain) + shift).astype(jnp.bfloat16)
        part = pl.ds(r * HALF, HALF)
        ffn_ref[0, part, :] = out[:HALF]
        ffn_ref[1, part, :] = out[HALF:]

    for copy in [w_z, far_b, far_c, up, down, par_mid, par_top, par_bot, far_up, far_down]:
        copy.wait_send()
    for copy in w_x + w_yn + w_yf + w_c:
        copy.wait_send()
    for j in range(7):
        share(j).wait_send()

    def sent(k, carry):
        @pl.when(k < T_ROWS * (N_TA - 1 - g))
        def _():
            hop_r(k).wait_send()

        @pl.when(k < T_ROWS * g)
        def _():
            hop_l(k).wait_send()

        return carry

    lax.fori_loop(0, T_ROWS * (N_TA - 1), sent, 0)


def shards(hidden_states, queries, keys_values, out_weight, mod_table, windows, step_index):
    flat = (FRAMES, ROWS * COLS, FEAT)
    any_spec = pl.BlockSpec(memory_space=pl.ANY)
    smem_spec = pl.BlockSpec(memory_space=pltpu.SMEM)
    vmem_spec = pl.BlockSpec(memory_space=pltpu.VMEM)
    column = pltpu.VMEM((2, (T_ROWS + 2) * TOK, FEAT), jnp.bfloat16)
    tiles = T_ROWS * HEADS_HERE
    residual_out, ffn_input = pl.pallas_call(
        kernel,
        out_shape=[jax.ShapeDtypeStruct(flat, jnp.bfloat16)] * 2,
        in_specs=[smem_spec] * 2 + [any_spec] * 5,
        out_specs=[vmem_spec] * 2,
        scratch_shapes=[
            column,
            column,
            column,
            pltpu.VMEM((D, FEAT), jnp.bfloat16),
            pltpu.VMEM(flat, jnp.bfloat16),
            pltpu.VMEM(flat, jnp.bfloat16),
            pltpu.VMEM(mod_table.shape, jnp.float32),
            pltpu.VMEM((TOKENS, FEAT), jnp.bfloat16),
            pltpu.VMEM((tiles, TOK, HD), jnp.float32),
            pltpu.VMEM((tiles, TOK, HD), jnp.float32),
            pltpu.VMEM((tiles, TOK, HD), jnp.float32),
            pltpu.VMEM((N_PIECE, TOK, FEAT), jnp.bfloat16),
            pltpu.VMEM((N_PIECE, TOK, FEAT), jnp.bfloat16),
            pltpu.VMEM((TOKENS, FEAT), jnp.float32),
            pltpu.VMEM((N_TA, 8, TOKENS), jnp.float32),
            pltpu.SemaphoreType.DMA((10,)),
            pltpu.SemaphoreType.DMA((28,)),
            pltpu.SemaphoreType.DMA((28,)),
            pltpu.SemaphoreType.DMA((N_PIECE,)),
            pltpu.SemaphoreType.DMA((N_PIECE,)),
            pltpu.SemaphoreType.DMA((N_PIECE,)),
            pltpu.SemaphoreType.DMA((N_PIECE,)),
            pltpu.SemaphoreType.DMA((7,)),
            pltpu.SemaphoreType.DMA((7,)),
        ],
        compiler_params=pltpu.CompilerParams(
            collective_id=0, has_side_effects=True, vmem_limit_bytes=52 * 2**20
        ),
    )(
        windows,
        step_index,
        hidden_states.reshape(flat),
        queries.reshape(flat),
        keys_values.reshape((2,) + flat),
        out_weight.T,
        mod_table,
    )
    shape = (FRAMES, ROWS, COLS, FEAT)
    return residual_out.reshape(shape), ffn_input.reshape(shape)


def solution(mesh):
    return jax.shard_map(
        shards,
        mesh=mesh,
        in_specs=(
            P(None, "ha", "wa", "ta"),
            P(None, "ha", "wa", "ta"),
            P(None, None, "ha", "wa", "ta"),
            P("ta", "wa"),
            P(None, None, "ta"),
            P("ta", None),
            P(),
        ),
        out_specs=(P(None, "ha", "wa", "ta"), P(None, "ha", "wa", "ta")),
        check_vma=False,
    )
```

time: 445 us -> 214 us (0.48)
  the two profiles are of different devices: /device:TPU:2 before, /device:TPU:9 now
where the time goes in v1:
time: 214 us
  Pallas kernels  208 us (97%)
  local copies, waits for them, and re-layouts  4.3 us (2%)
    pallas_call x1, Pallas kernels, shards(): pl.pallas_call(kernel, out_shape=[jax.ShapeDtypeStruct(flat, jnp.bfloat16...  208 us
    unnamed x8, local copies, waits for them, and re-layouts  4.3 us

profile of v1, /device:TPU:9, one launch (start us, length us, event | category | flops | bytes accessed | tf_op | source)
XLA Modules:
  0.0 213.9 jit_solution(5837831002924499521)
XLA Ops:
  0.6 0.0 copy-start
  1.3 0.8 copy.9.win_ref
  2.1 0.0 copy-start.1
  2.1 2.0 copy.10.mod_ref
  4.1 0.0 copy-done
  4.1 0.0 copy-done.1
  4.1 208.3 %shard_map.86 = (bf16[2,192,640]{2,1,0:T(8,128)(2,1)S(1)}, bf16[2,192,640]{2,1,0:T(8,128)(2,1)S(1)}) custom-call(s32[5,2]{1,0:T(8,128)S(1)} %copy.9.win_ref, s32[1]{0:T(128)S(6)} %copy.13.step_ref, bf16[2,192,640]{2,1,0:T(8,128)(2,1)S(1)} %bitcast.6, bf16[2,192,640]{2,1,0:T(8,128)(2,1)} %bitcast.11, bf16[2,2,192,640]{3,2,1,0:T(8,128)(2,1)} %bitcast.10, ...), custom_call_target="tpu_custom_call" | custom-call | tf_op jit(solution)/shard_map/pallas_call | solution.py:438
  212.3 0.8 copy.14
  213.1 0.8 copy.15
Async XLA Ops:
  0.6 3.4 %copy-start = (bf16[2,24,8,640]{3,2,1,0:T(8,128)(2,1)S(1)}, bf16[2,24,8,640]{3,2,1,0:T(8,128)(2,1)}, u32[]{:S(2)}) copy-start(bf16[2,24,8,640]{3,2,1,0:T(8,128)(2,1)} %param.7) | copy-start | bytes 1474564
  2.1 2.0 copy-start.1

commit v2 on v1

--- a/solution.py
+++ b/solution.py
@@ -75,6 +75,8 @@
     dev_par = (x, 4 * y + 2 * zh + 1 - c, g)
     dev_far = (x, lax.rem(wa + 15 + 2 * c, 16), g)
     dev_z = (x, nw, g)
+    dev_diag = (x, 4 * y + 2 * (1 - zh) + 1 - c, g)
+    dev_via = (x, 15 * (wa // 8), g)
     dev_x = [(lax.rem(x + j + 1, N_HA), wa, g) for j in range(3)]
     dev_y = [(x, lax.rem(wa + 4 * (j + 1), 16), g) for j in range(3)]
     dev_t = [(x, wa, lax.rem(g + j + 1, N_TA)) for j in range(7)]
@@ -84,6 +86,11 @@
 
     def quarter_rows(index, part):
         return pl.ds(pl.multiple_of(index * SHARD + part * QUARTER, QUARTER), QUARTER)
+
+    is_relay = (wa == 0) | (wa == N_WA - 1)
+    has_far = (wa > 0) & (wa < N_WA - 1)
+    is_via = (wa == 4) | (wa == 11)
+    is_direct = has_far & (wa != 4) & (wa != 11)
 
     loads = []
     for f in range(FRAMES):
@@ -106,6 +113,10 @@
     load_h.start()
     load_m.start()
 
+    @pl.when(is_relay)
+    def _():
+        far[...] = jnp.zeros_like(far)
+
     @pl.when(g == 0)
     def _():
         slot_r[...] = jnp.zeros_like(slot_r)
@@ -115,7 +126,7 @@
         slot_l[...] = jnp.zeros_like(slot_l)
 
     barrier = pltpu.get_barrier_semaphore()
-    peers = [dev_par, dev_far, dev_z] + dev_x + dev_y + dev_t
+    peers = [dev_par, dev_far, dev_z, dev_diag] + dev_x + dev_y + dev_t
     for peer in peers:
         pl.semaphore_signal(barrier, inc=1, device_id=peer, device_id_type=MESH)
     for load in loads:
@@ -138,8 +149,18 @@
 
     w_z = remote(0, wall.at[quarter_rows(wa, x)], wall.at[quarter_rows(wa, x)], dev_z)
     far_a = remote(1, rows(own, 1, 1), rows(far, 1, 1), dev_far)
-    far_b = remote(2, rows(own, 3, 1), rows(far, 3, 1), dev_far)
-    far_c = remote(3, rows(own, 2, 1), rows(far, 2, 1), dev_far)
+    def far_rows_b(src, device):
+        return remote(2, rows(src, 3, 1), rows(far, 3, 1), device)
+
+    def middle(buf, head):
+        return buf.at[:, pl.ds(2 * TOK, TOK), pl.ds(head * HD, HD)]
+
+    def far_head(head, src, device):
+        return remote(28 + head, middle(src, head), middle(far, head), device)
+
+    far_b = far_rows_b(own, dev_far)
+    far_c = [far_head(head, own, dev_far) for head in range(HEADS_HERE)]
+    passed = range(3, HEADS_HERE)
     up = remote(4, rows(own, 1, 1), rows(own, 4, 1), dev_x[2])
     down = remote(5, rows(own, 3, 1), rows(own, 0, 1), dev_x[0])
     par_mid = remote(6, rows(own, 1, 3), rows(par, 1, 3), dev_par)
@@ -169,8 +190,21 @@
         w_c.append(remote(25 + j, wall.at[shard_rows(other)], wall.at[shard_rows(other)], dev_par))
 
     w_z.start()
-    far_a.start()
-    far_b.start()
+
+    @pl.when(has_far)
+    def _():
+        far_a.start()
+
+    @pl.when(is_direct)
+    def _():
+        far_b.start()
+
+    @pl.when(is_via)
+    def _():
+        far_rows_b(own, dev_via).start()
+        for head in passed:
+            far_head(head, own, dev_via).start()
+
     up.start()
     down.start()
     par_mid.start()
@@ -195,12 +229,18 @@
     par_top.wait_recv()
     par_bot.wait_recv()
     load_q.wait()
+
+    @pl.when(is_relay)
+    def _():
+        far_b.wait_recv()
+        far_rows_b(far, dev_diag).start()
+
     scale = 1.0 / math.sqrt(HD)
     far_there = jnp.where(c == 0, wa > 0, wa < N_WA - 1)
 
     def biases(r, head, beside, there):
-        radius_row = win_ref[head, 0]
-        radius_col = win_ref[head, 1]
+        radius_row = win_ref[0, head]
+        radius_col = win_ref[1, head]
         out = []
         for gap in (-1, 0, 1):
             row = T_ROWS * x + r + gap
@@ -214,10 +254,10 @@
         return pl.ds(pl.multiple_of(head * HD, HD), HD)
 
     def token_rows(r, count):
-        return pl.ds(pl.multiple_of(r * TOK, TOK), count * TOK)
+        return pl.ds(r * TOK if isinstance(r, int) else pl.multiple_of(r * TOK, TOK), count * TOK)
 
     def query_tile(r, head):
-        part = pl.ds(pl.multiple_of(r * HALF, HALF), HALF)
+        part = pl.ds(r * HALF if isinstance(r, int) else pl.multiple_of(r * HALF, HALF), HALF)
         return jnp.concatenate([qry[0, part, lanes(head)], qry[1, part, lanes(head)]], axis=0)
 
     def scores(query, buf, r, head, bias):
@@ -255,25 +295,48 @@
 
     lax.fori_loop(0, T_ROWS * HEADS_HERE, near_tile, 0)
 
-    far_a.wait_send()
-    far_c.start()
-    far_a.wait_recv()
-    far_up.start()
+    @pl.when(has_far)
+    def _():
+        far_a.wait_send()
+        for head in range(3):
+            far_c[head].start()
+
+    @pl.when(is_direct)
+    def _():
+        for head in passed:
+            far_c[head].start()
+
+    @pl.when(is_relay)
+    def _():
+        for head in passed:
+            far_c[head].wait_recv()
+            far_head(head, far, dev_diag).start()
+
+    @pl.when(has_far)
+    def _():
+        far_a.wait_recv()
+        far_up.start()
+
     for j in range(3):
         w_yn[j].wait_recv()
         w_c[2 + j].start()
-    far_b.wait_recv()
-    far_down.start()
+
+    @pl.when(has_far)
+    def _():
+        far_b.wait_recv()
+        far_down.start()
+
     for j in range(3):
         w_yf[j].wait_recv()
         w_c[5 + j].start()
-    far_up.wait_recv()
-    far_down.wait_recv()
-    far_c.wait_recv()
-
-    def far_tile(index, carry):
-        r = index // HEADS_HERE
-        head = lax.rem(index, HEADS_HERE)
+
+    @pl.when(has_far)
+    def _():
+        far_up.wait_recv()
+        far_down.wait_recv()
+
+    def far_tile(r, head):
+        index = r * HEADS_HERE + head
         query = query_tile(r, head)
         s_far = scores(query, far, r, head, biases(r, head, True, far_there))
         before = m_part[index]
@@ -285,9 +348,24 @@
         norm = shrink * l_part[index] + jnp.sum(total(p_far, jnp.add), axis=1, keepdims=True)
         out = (shrink * o_part[index] + values(p_far, far, r, head)) / norm
         att[token_rows(r, 1), lanes(head)] = out.astype(jnp.bfloat16)
+
+    def far_step(head, carry):
+        @pl.when(has_far)
+        def _():
+            pltpu.make_async_remote_copy(
+                src_ref=middle(own, 0),
+                dst_ref=middle(far, 0),
+                send_sem=ssem.at[28 + head],
+                recv_sem=rsem.at[28 + head],
+                device_id=dev_far,
+                device_id_type=MESH,
+            ).wait_recv()
+
+        for r in range(T_ROWS):
+            far_tile(r, head)
         return carry
 
-    lax.fori_loop(0, T_ROWS * HEADS_HERE, far_tile, 0)
+    lax.fori_loop(0, HEADS_HERE, far_step, 0)
     for copy in w_c:
         copy.wait_recv()
 
@@ -351,9 +429,19 @@
 
     load_h.wait()
     load_m.wait()
-    picked = mod[step_ref[0]]
-    gate, shift, gain = picked[0:1], picked[1:2], picked[2:3]
+    gate, shift, gain = [mod[j, pl.ds(step_ref[0], 1), :] for j in range(3)]
     lane = lax.broadcasted_iota(jnp.int32, (TOK, HD), 1)
+
+    def share(j, r):
+        return pltpu.make_async_remote_copy(
+            src_ref=stat.at[0, r],
+            dst_ref=stat.at[j + 1, r],
+            send_sem=ssem_s.at[j * T_ROWS + r],
+            recv_sem=rsem_s.at[j * T_ROWS + r],
+            device_id=dev_t[j],
+            device_id_type=MESH,
+        )
+
     for r in range(T_ROWS):
         own_part = partial_sum(g, r)
         k = T_ROWS * (N_TA - 1 - g) + r
@@ -378,25 +466,14 @@
         first = jnp.sum(now, axis=1, keepdims=True)
         second = jnp.sum(now * now, axis=1, keepdims=True)
         both = jnp.where(lane == 0, first, jnp.where(lane == 1, second, 0.0))
-        stat[0, :, pl.ds(r * TOK, TOK)] = jnp.transpose(both)[:8]
-
-    def share(j):
-        return pltpu.make_async_remote_copy(
-            src_ref=stat.at[0],
-            dst_ref=stat.at[j + 1],
-            send_sem=ssem_s.at[j],
-            recv_sem=rsem_s.at[j],
-            device_id=dev_t[j],
-            device_id_type=MESH,
-        )
-
-    for j in range(7):
-        share(j).start()
-    for j in range(7):
-        share(j).wait_recv()
-    sums = total([stat[j] for j in range(N_TA)], jnp.add)
+        stat[0, r] = jnp.transpose(both)[:8]
+        for j in range(7):
+            share(j, r).start()
+
     for r in range(T_ROWS):
-        line = sums[:, r * TOK : (r + 1) * TOK]
+        for j in range(7):
+            share(j, r).wait_recv()
+        line = total([stat[j, r] for j in range(N_TA)], jnp.add)
         column = jnp.transpose(jnp.concatenate([line] * (HD // 8), axis=0))
         average = column[:, 0:1] / D
         variance = column[:, 1:2] / D - average * average
@@ -407,12 +484,21 @@
         ffn_ref[0, part, :] = out[:HALF]
         ffn_ref[1, part, :] = out[HALF:]
 
-    for copy in [w_z, far_b, far_c, up, down, par_mid, par_top, par_bot, far_up, far_down]:
+    for copy in [w_z, far_b, up, down, par_mid, par_top, par_bot]:
         copy.wait_send()
+    for head in passed:
+        far_c[head].wait_send()
+
+    @pl.when(has_far)
+    def _():
+        for copy in [far_up, far_down] + far_c[:3]:
+            copy.wait_send()
+
     for copy in w_x + w_yn + w_yf + w_c:
         copy.wait_send()
     for j in range(7):
-        share(j).wait_send()
+        for r in range(T_ROWS):
+            share(j, r).wait_send()
 
     def sent(k, carry):
         @pl.when(k < T_ROWS * (N_TA - 1 - g))
@@ -447,7 +533,7 @@
             pltpu.VMEM((D, FEAT), jnp.bfloat16),
             pltpu.VMEM(flat, jnp.bfloat16),
             pltpu.VMEM(flat, jnp.bfloat16),
-            pltpu.VMEM(mod_table.shape, jnp.float32),
+            pltpu.VMEM((3, mod_table.shape[0], FEAT), jnp.float32),
             pltpu.VMEM((TOKENS, FEAT), jnp.bfloat16),
             pltpu.VMEM((tiles, TOK, HD), jnp.float32),
             pltpu.VMEM((tiles, TOK, HD), jnp.float32),
@@ -455,28 +541,28 @@
             pltpu.VMEM((N_PIECE, TOK, FEAT), jnp.bfloat16),
             pltpu.VMEM((N_PIECE, TOK, FEAT), jnp.bfloat16),
             pltpu.VMEM((TOKENS, FEAT), jnp.float32),
-            pltpu.VMEM((N_TA, 8, TOKENS), jnp.float32),
+            pltpu.VMEM((N_TA, T_ROWS, 8, HD), jnp.float32),
             pltpu.SemaphoreType.DMA((10,)),
-            pltpu.SemaphoreType.DMA((28,)),
-            pltpu.SemaphoreType.DMA((28,)),
+            pltpu.SemaphoreType.DMA((33,)),
+            pltpu.SemaphoreType.DMA((33,)),
             pltpu.SemaphoreType.DMA((N_PIECE,)),
             pltpu.SemaphoreType.DMA((N_PIECE,)),
             pltpu.SemaphoreType.DMA((N_PIECE,)),
             pltpu.SemaphoreType.DMA((N_PIECE,)),
-            pltpu.SemaphoreType.DMA((7,)),
-            pltpu.SemaphoreType.DMA((7,)),
+            pltpu.SemaphoreType.DMA((7 * T_ROWS,)),
+            pltpu.SemaphoreType.DMA((7 * T_ROWS,)),
         ],
         compiler_params=pltpu.CompilerParams(
             collective_id=0, has_side_effects=True, vmem_limit_bytes=52 * 2**20
         ),
     )(
-        windows,
+        windows.T,
         step_index,
         hidden_states.reshape(flat),
         queries.reshape(flat),
         keys_values.reshape((2,) + flat),
         out_weight.T,
-        mod_table,
+        mod_table.transpose(1, 0, 2),
     )
     shape = (FRAMES, ROWS, COLS, FEAT)
     return residual_out.reshape(shape), ffn_input.reshape(shape)

time: 214 us -> 198 us (0.925)
  the two profiles are of different devices: /device:TPU:9 before, /device:TPU:12 now
where the time goes in v2:
time: 198 us
  Pallas kernels  193 us (97%)
  local copies, waits for them, and re-layouts  4.24 us (2%)
    pallas_call x1, Pallas kernels, shards(): pl.pallas_call(kernel, out_shape=[jax.ShapeDtypeStruct(flat, jnp.bfloat16...  193 us
    unnamed x8, local copies, waits for them, and re-layouts  4.24 us

profile of v2, /device:TPU:12, one launch (start us, length us, event | category | flops | bytes accessed | tf_op | source)
XLA Modules:
  0.0 198.2 jit_solution(4527103375281865977)
XLA Ops:
  1.3 0.0 copy-start.2
  1.3 0.7 copy-done.2
  2.0 0.0 copy-start
  2.0 1.0 copy-done
  3.0 0.0 copy-start.1
  3.0 1.0 copy-done.1
  4.0 192.7 %shard_map.86 = (bf16[2,192,640]{2,1,0:T(8,128)(2,1)S(1)}, bf16[2,192,640]{2,1,0:T(8,128)(2,1)S(1)}) custom-call(s32[2,5]{1,0:T(2,128)S(1)} %bitcast.12, s32[1]{0:T(128)S(6)} %copy.11.step_ref, bf16[2,192,640]{2,1,0:T(8,128)(2,1)} %bitcast.14, bf16[2,192,640]{2,1,0:T(8,128)(2,1)} %bitcast.15, bf16[2,2,192,640]{3,2,1,0:T(8,128)(2,1)} %bitcast.13, ...), custom_call_target="tpu_custom_call" | custom-call | tf_op jit(solution)/shard_map/pallas_call | solution.py:524
  196.7 0.8 copy.12
  197.5 0.8 copy.13
Async XLA Ops:
  1.3 0.7 copy-start.2
  2.0 1.0 copy-start
  3.0 1.0 copy-start.1

commit v3 on v2

--- a/solution.py
+++ b/solution.py
@@ -50,6 +50,7 @@
     o_part,
     m_part,
     l_part,
+    wext,
     slot_r,
     slot_l,
     mixed,
@@ -57,6 +58,8 @@
     lsem,
     ssem,
     rsem,
+    ssem_e,
+    rsem_e,
     ssem_r,
     rsem_r,
     ssem_l,
@@ -80,6 +83,12 @@
     dev_x = [(lax.rem(x + j + 1, N_HA), wa, g) for j in range(3)]
     dev_y = [(x, lax.rem(wa + 4 * (j + 1), 16), g) for j in range(3)]
     dev_t = [(x, wa, lax.rem(g + j + 1, N_TA)) for j in range(7)]
+
+    is_end = (g == 0) | (g == N_TA - 1)
+    is_next = (g == 1) | (g == N_TA - 2)
+    upper = g // (N_TA // 2)
+    ext_y = (N_Y - 1) * (1 - upper)
+    dev_next = (x, wa, 1 + (N_TA - 3) * upper)
 
     def shard_rows(index):
         return pl.ds(pl.multiple_of(index * SHARD, SHARD), SHARD)
@@ -119,11 +128,11 @@
 
     @pl.when(g == 0)
     def _():
-        slot_r[...] = jnp.zeros_like(slot_r)
+        slot_r[N_PIECE - T_ROWS :] = jnp.zeros((T_ROWS, TOK, FEAT), jnp.bfloat16)
 
     @pl.when(g == N_TA - 1)
     def _():
-        slot_l[...] = jnp.zeros_like(slot_l)
+        slot_l[N_PIECE - T_ROWS :] = jnp.zeros((T_ROWS, TOK, FEAT), jnp.bfloat16)
 
     barrier = pltpu.get_barrier_semaphore()
     peers = [dev_par, dev_far, dev_z, dev_diag] + dev_x + dev_y + dev_t
@@ -189,7 +198,44 @@
         other = lax.rem(nw + 4 * (3 - j), 16)
         w_c.append(remote(25 + j, wall.at[shard_rows(other)], wall.at[shard_rows(other)], dev_par))
 
+    def ext_quarter(half, part):
+        return wext.at[pl.ds(pl.multiple_of((2 * half + c) * SHARD + part * QUARTER, QUARTER), QUARTER)]
+
+    def ext_shard(half):
+        return wext.at[pl.ds(pl.multiple_of((2 * half + c) * SHARD, SHARD), SHARD)]
+
+    def ext(send, recv, src, dst, device):
+        return pltpu.make_async_remote_copy(
+            src_ref=src,
+            dst_ref=dst,
+            send_sem=ssem_e.at[send],
+            recv_sem=rsem_e.at[recv],
+            device_id=device,
+            device_id_type=MESH,
+        )
+
+    ext_t = ext(0, 0, wall.at[quarter_rows(wa, x)], ext_quarter(zh, x), dev_next)
+    ext_z = ext(0, 1, ext_quarter(zh, x), ext_quarter(zh, x), dev_z)
+    ext_y_copies = [
+        ext(1 + 2 * j + n, n, ext_quarter(half, x), ext_quarter(half, x), dev_y[j])
+        for j in range(3)
+        for n, half in ((0, zh), (1, 1 - zh))
+    ]
+    ext_x_copies = [
+        ext(7 + 2 * j + n, 2 + 2 * j + n, ext_quarter(half, x), ext_quarter(half, x), dev_x[j])
+        for j in range(3)
+        for n, half in ((0, zh), (1, 1 - zh))
+    ]
+    ext_c_copies = [
+        ext(13 + n, 8 + n, ext_shard(half), ext_shard(half), dev_par)
+        for n, half in ((0, zh), (1, 1 - zh))
+    ]
+
     w_z.start()
+
+    @pl.when(is_end & (y == ext_y))
+    def _():
+        ext_t.start()
 
     @pl.when(has_far)
     def _():
@@ -234,6 +280,12 @@
     def _():
         far_b.wait_recv()
         far_rows_b(far, dev_diag).start()
+
+
+    @pl.when(is_next & (y == ext_y))
+    def _():
+        ext_t.wait_recv()
+        ext_z.start()
 
     scale = 1.0 / math.sqrt(HD)
     far_there = jnp.where(c == 0, wa > 0, wa < N_WA - 1)
@@ -312,6 +364,12 @@
             far_c[head].wait_recv()
             far_head(head, far, dev_diag).start()
 
+    @pl.when(is_next & (y == ext_y))
+    def _():
+        ext_z.wait_recv()
+        for copy in ext_y_copies:
+            copy.start()
+
     @pl.when(has_far)
     def _():
         far_a.wait_recv()
@@ -321,6 +379,16 @@
         w_yn[j].wait_recv()
         w_c[2 + j].start()
 
+    @pl.when(is_next)
+    def _():
+        @pl.when(y != ext_y)
+        def _():
+            for copy in ext_y_copies[:2]:
+                copy.wait_recv()
+
+        for copy in ext_x_copies:
+            copy.start()
+
     @pl.when(has_far)
     def _():
         far_b.wait_recv()
@@ -329,6 +397,13 @@
     for j in range(3):
         w_yf[j].wait_recv()
         w_c[5 + j].start()
+
+    @pl.when(is_next)
+    def _():
+        for copy in ext_x_copies:
+            copy.wait_recv()
+        for copy in ext_c_copies:
+            copy.start()
 
     @pl.when(has_far)
     def _():
@@ -369,6 +444,11 @@
     for copy in w_c:
         copy.wait_recv()
 
+    @pl.when(is_next)
+    def _():
+        for copy in ext_c_copies:
+            copy.wait_recv()
+
     right = (x, wa, lax.rem(g + 1, N_TA))
     left = (x, wa, lax.rem(g + N_TA - 1, N_TA))
 
@@ -378,54 +458,77 @@
             att[token_rows(r, 1), :], weight, NT, preferred_element_type=jnp.float32
         )
 
-    def hop_r(k):
-        return pltpu.make_async_remote_copy(
-            src_ref=slot_r.at[k],
-            dst_ref=slot_r.at[k],
-            send_sem=ssem_r.at[k],
-            recv_sem=rsem_r.at[k],
-            device_id=right,
-            device_id_type=MESH,
-        )
-
-    def hop_l(k):
-        return pltpu.make_async_remote_copy(
-            src_ref=slot_l.at[k],
-            dst_ref=slot_l.at[k],
-            send_sem=ssem_l.at[k],
-            recv_sem=rsem_l.at[k],
-            device_id=left,
-            device_id_type=MESH,
-        )
-
-    def hop(tau, carry):
+    def extra_sum(taken, far_dest):
+        weight = wext[pl.ds(pl.multiple_of(far_dest * FEAT, FEAT), FEAT), :]
+        return lax.dot_general(taken, weight, NT, preferred_element_type=jnp.float32)
+
+    def flow(slots, send, recv, device):
+        def hop(src, k):
+            return pltpu.make_async_remote_copy(
+                src_ref=src,
+                dst_ref=slots.at[k],
+                send_sem=send.at[k],
+                recv_sem=recv.at[k],
+                device_id=device,
+                device_id_type=MESH,
+            )
+
+        return hop
+
+    hop_r = flow(slot_r, ssem_r, rsem_r, right)
+    hop_l = flow(slot_l, ssem_l, rsem_l, left)
+
+    def step(hop, slots, k, place, dest_of, ext_of):
+        r = lax.rem(k, T_ROWS)
+        taken = 2 * T_ROWS
+
+        @pl.when((place == 0) & (k < T_ROWS))
+        def _():
+            hop(att.at[token_rows(r, 1)], k).start()
+
+        @pl.when((place == 0) & (k >= taken))
+        def _():
+            slots[k] = partial_sum(dest_of(k), r).astype(jnp.bfloat16)
+            hop(slots.at[k], k).start()
+
+        @pl.when((place == 1) & (k < T_ROWS))
+        def _():
+            hop(slots.at[k], k).wait_recv()
+            add = partial_sum(dest_of(k), r) + extra_sum(slots[k], ext_of(k))
+            slots[N_PIECE - T_ROWS + r] = add.astype(jnp.bfloat16)
+            hop(slots.at[N_PIECE - T_ROWS + r], k).start()
+
+        @pl.when((place == 1) & (k >= T_ROWS) & (k < taken))
+        def _():
+            add = partial_sum(dest_of(k), r) + extra_sum(slots[r], ext_of(k))
+            slots[k] = add.astype(jnp.bfloat16)
+            hop(slots.at[k], k).start()
+
+        @pl.when((place > 1) | ((place == 1) & (k >= taken)))
+        def _():
+            hop(slots.at[k], k).wait_recv()
+            add = partial_sum(dest_of(k), r)
+            slots[k] = (slots[k].astype(jnp.float32) + add).astype(jnp.bfloat16)
+            hop(slots.at[k], k).start()
+
+    def hops(tau, carry):
         k = tau - 2 * g
 
         @pl.when((k >= 0) & (k < T_ROWS * (N_TA - 1 - g)))
         def _():
-            @pl.when(g > 0)
-            def _():
-                hop_r(k).wait_recv()
-
-            add = partial_sum(N_TA - 1 - k // T_ROWS, lax.rem(k, T_ROWS))
-            slot_r[k] = (slot_r[k].astype(jnp.float32) + add).astype(jnp.bfloat16)
-            hop_r(k).start()
+            step(
+                hop_r, slot_r, k, g, lambda m: N_TA - 1 - m // T_ROWS, lambda m: 1 - m // T_ROWS
+            )
 
         n = tau - 2 * (N_TA - 1 - g)
 
         @pl.when((n >= 0) & (n < T_ROWS * g))
         def _():
-            @pl.when(g < N_TA - 1)
-            def _():
-                hop_l(n).wait_recv()
-
-            add = partial_sum(n // T_ROWS, lax.rem(n, T_ROWS))
-            slot_l[n] = (slot_l[n].astype(jnp.float32) + add).astype(jnp.bfloat16)
-            hop_l(n).start()
+            step(hop_l, slot_l, n, N_TA - 1 - g, lambda m: m // T_ROWS, lambda m: m // T_ROWS)
 
         return carry
 
-    lax.fori_loop(0, T_ROWS * (N_TA - 1), hop, 0)
+    lax.fori_loop(0, T_ROWS * (N_TA - 1), hops, 0)
 
     load_h.wait()
     load_m.wait()
@@ -449,11 +552,11 @@
 
         @pl.when(g > 0)
         def _():
-            hop_r(k).wait_recv()
+            hop_r(slot_r.at[k], k).wait_recv()
 
         @pl.when(g < N_TA - 1)
         def _():
-            hop_l(n).wait_recv()
+            hop_l(slot_l.at[n], n).wait_recv()
 
         projected = own_part + slot_r[k].astype(jnp.float32) + slot_l[n].astype(jnp.float32)
         part = pl.ds(r * HALF, HALF)
@@ -500,14 +603,30 @@
         for r in range(T_ROWS):
             share(j, r).wait_send()
 
+    @pl.when(is_end & (y == ext_y))
+    def _():
+        ext_t.wait_send()
+
+    @pl.when(is_next)
+    def _():
+        @pl.when(y == ext_y)
+        def _():
+            for copy in [ext_z] + ext_y_copies:
+                copy.wait_send()
+
+        for copy in ext_x_copies + ext_c_copies:
+            copy.wait_send()
+
     def sent(k, carry):
-        @pl.when(k < T_ROWS * (N_TA - 1 - g))
-        def _():
-            hop_r(k).wait_send()
-
-        @pl.when(k < T_ROWS * g)
-        def _():
-            hop_l(k).wait_send()
+        left_out = (k >= T_ROWS) & (k < 2 * T_ROWS)
+
+        @pl.when((k < T_ROWS * (N_TA - 1 - g)) & ~((g == 0) & left_out))
+        def _():
+            hop_r(slot_r.at[k], k).wait_send()
+
+        @pl.when((k < T_ROWS * g) & ~((g == N_TA - 1) & left_out))
+        def _():
+            hop_l(slot_l.at[k], k).wait_send()
 
         return carry
 
@@ -538,6 +657,7 @@
             pltpu.VMEM((tiles, TOK, HD), jnp.float32),
             pltpu.VMEM((tiles, TOK, HD), jnp.float32),
             pltpu.VMEM((tiles, TOK, HD), jnp.float32),
+            pltpu.VMEM((4 * SHARD, FEAT), jnp.bfloat16),
             pltpu.VMEM((N_PIECE, TOK, FEAT), jnp.bfloat16),
             pltpu.VMEM((N_PIECE, TOK, FEAT), jnp.bfloat16),
             pltpu.VMEM((TOKENS, FEAT), jnp.float32),
@@ -545,6 +665,8 @@
             pltpu.SemaphoreType.DMA((10,)),
             pltpu.SemaphoreType.DMA((33,)),
             pltpu.SemaphoreType.DMA((33,)),
+            pltpu.SemaphoreType.DMA((15,)),
+            pltpu.SemaphoreType.DMA((10,)),
             pltpu.SemaphoreType.DMA((N_PIECE,)),
             pltpu.SemaphoreType.DMA((N_PIECE,)),
             pltpu.SemaphoreType.DMA((N_PIECE,)),
@@ -553,7 +675,7 @@
             pltpu.SemaphoreType.DMA((7 * T_ROWS,)),
         ],
         compiler_params=pltpu.CompilerParams(
-            collective_id=0, has_side_effects=True, vmem_limit_bytes=52 * 2**20
+            collective_id=0, has_side_effects=True, vmem_limit_bytes=60 * 2**20
         ),
     )(
         windows.T,

time: 198 us -> 221 us (1.12)
  the two profiles are of different devices: /device:TPU:12 before, /device:TPU:16 now
where the time goes in v3:
time: 221 us
  Pallas kernels  217 us (98%)
  local copies, waits for them, and re-layouts  2.69 us (1%)
    pallas_call x1, Pallas kernels, shards(): pl.pallas_call(kernel, out_shape=[jax.ShapeDtypeStruct(flat, jnp.bfloat16...  217 us

profile of v3, /device:TPU:16, one launch (start us, length us, event | category | flops | bytes accessed | tf_op | source)
XLA Modules:
  0.0 221.0 jit_solution(13256273447702079723)
XLA Ops:
  1.3 217.0 %shard_map.86 = (bf16[2,192,640]{2,1,0:T(8,128)(2,1)}, bf16[2,192,640]{2,1,0:T(8,128)(2,1)}) custom-call(s32[2,5]{1,0:T(2,128)} %bitcast.15, s32[1]{0:T(128)S(6)} %copy.11.step_ref, bf16[2,192,640]{2,1,0:T(8,128)(2,1)} %bitcast.9, bf16[2,192,640]{2,1,0:T(8,128)(2,1)} %bitcast.10, bf16[2,2,192,640]{3,2,1,0:T(8,128)(2,1)} %bitcast.8, ...), custom_call_target="tpu_custom_call" | custom-call | tf_op jit(solution)/shard_map/pallas_call | solution.py:643
  218.3 0.0 copy-start
  218.3 1.9 copy.12
  220.2 0.0 copy-done
  220.2 0.8 copy.13
Async XLA Ops:
  218.3 1.9 copy-start

commit v4 on v3

--- a/solution.py
+++ b/solution.py
@@ -89,6 +89,8 @@
     upper = g // (N_TA // 2)
     ext_y = (N_Y - 1) * (1 - upper)
     dev_next = (x, wa, 1 + (N_TA - 3) * upper)
+    dev_cross = (x, nw, 1 + (N_TA - 3) * upper)
+    dev_beside = (x, nw, g + 1 - 2 * lax.rem(g, 2))
 
     def shard_rows(index):
         return pl.ds(pl.multiple_of(index * SHARD, SHARD), SHARD)
@@ -135,7 +137,7 @@
         slot_l[N_PIECE - T_ROWS :] = jnp.zeros((T_ROWS, TOK, FEAT), jnp.bfloat16)
 
     barrier = pltpu.get_barrier_semaphore()
-    peers = [dev_par, dev_far, dev_z, dev_diag] + dev_x + dev_y + dev_t
+    peers = [dev_par, dev_far, dev_z, dev_diag, dev_beside] + dev_x + dev_y + dev_t
     for peer in peers:
         pl.semaphore_signal(barrier, inc=1, device_id=peer, device_id_type=MESH)
     for load in loads:
@@ -215,19 +217,19 @@
         )
 
     ext_t = ext(0, 0, wall.at[quarter_rows(wa, x)], ext_quarter(zh, x), dev_next)
-    ext_z = ext(0, 1, ext_quarter(zh, x), ext_quarter(zh, x), dev_z)
+    ext_z = ext(1, 1, wall.at[quarter_rows(wa, x)], ext_quarter(zh, x), dev_cross)
     ext_y_copies = [
-        ext(1 + 2 * j + n, n, ext_quarter(half, x), ext_quarter(half, x), dev_y[j])
+        ext(2 + 2 * j + n, n, ext_quarter(half, x), ext_quarter(half, x), dev_y[j])
         for j in range(3)
         for n, half in ((0, zh), (1, 1 - zh))
     ]
     ext_x_copies = [
-        ext(7 + 2 * j + n, 2 + 2 * j + n, ext_quarter(half, x), ext_quarter(half, x), dev_x[j])
+        ext(8 + 2 * j + n, 2 + 2 * j + n, ext_quarter(half, x), ext_quarter(half, x), dev_x[j])
         for j in range(3)
         for n, half in ((0, zh), (1, 1 - zh))
     ]
     ext_c_copies = [
-        ext(13 + n, 8 + n, ext_shard(half), ext_shard(half), dev_par)
+        ext(14 + n, 8 + n, ext_shard(half), ext_shard(half), dev_par)
         for n, half in ((0, zh), (1, 1 - zh))
     ]
 
@@ -236,6 +238,7 @@
     @pl.when(is_end & (y == ext_y))
     def _():
         ext_t.start()
+        ext_z.start()
 
     @pl.when(has_far)
     def _():
@@ -271,6 +274,13 @@
     for copy in w_yf:
         copy.start()
 
+    @pl.when(is_next & (y == ext_y))
+    def _():
+        ext_t.wait_recv()
+        ext_z.wait_recv()
+        for copy in ext_y_copies:
+            copy.start()
+
     par_mid.wait_recv()
     par_top.wait_recv()
     par_bot.wait_recv()
@@ -280,12 +290,6 @@
     def _():
         far_b.wait_recv()
         far_rows_b(far, dev_diag).start()
-
-
-    @pl.when(is_next & (y == ext_y))
-    def _():
-        ext_t.wait_recv()
-        ext_z.start()
 
     scale = 1.0 / math.sqrt(HD)
     far_there = jnp.where(c == 0, wa > 0, wa < N_WA - 1)
@@ -347,6 +351,16 @@
 
     lax.fori_loop(0, T_ROWS * HEADS_HERE, near_tile, 0)
 
+    @pl.when(is_next)
+    def _():
+        @pl.when(y != ext_y)
+        def _():
+            for copy in ext_y_copies[:2]:
+                copy.wait_recv()
+
+        for copy in ext_x_copies:
+            copy.start()
+
     @pl.when(has_far)
     def _():
         far_a.wait_send()
@@ -363,40 +377,6 @@
         for head in passed:
             far_c[head].wait_recv()
             far_head(head, far, dev_diag).start()
-
-    @pl.when(is_next & (y == ext_y))
-    def _():
-        ext_z.wait_recv()
-        for copy in ext_y_copies:
-            copy.start()
-
-    @pl.when(has_far)
-    def _():
-        far_a.wait_recv()
-        far_up.start()
-
-    for j in range(3):
-        w_yn[j].wait_recv()
-        w_c[2 + j].start()
-
-    @pl.when(is_next)
-    def _():
-        @pl.when(y != ext_y)
-        def _():
-            for copy in ext_y_copies[:2]:
-                copy.wait_recv()
-
-        for copy in ext_x_copies:
-            copy.start()
-
-    @pl.when(has_far)
-    def _():
-        far_b.wait_recv()
-        far_down.start()
-
-    for j in range(3):
-        w_yf[j].wait_recv()
-        w_c[5 + j].start()
 
     @pl.when(is_next)
     def _():
@@ -404,6 +384,24 @@
             copy.wait_recv()
         for copy in ext_c_copies:
             copy.start()
+
+    @pl.when(has_far)
+    def _():
+        far_a.wait_recv()
+        far_up.start()
+
+    for j in range(3):
+        w_yn[j].wait_recv()
+        w_c[2 + j].start()
+
+    @pl.when(has_far)
+    def _():
+        far_b.wait_recv()
+        far_down.start()
+
+    for j in range(3):
+        w_yf[j].wait_recv()
+        w_c[5 + j].start()
 
     @pl.when(has_far)
     def _():
@@ -606,12 +604,13 @@
     @pl.when(is_end & (y == ext_y))
     def _():
         ext_t.wait_send()
+        ext_z.wait_send()
 
     @pl.when(is_next)
     def _():
         @pl.when(y == ext_y)
         def _():
-            for copy in [ext_z] + ext_y_copies:
+            for copy in ext_y_copies:
                 copy.wait_send()
 
         for copy in ext_x_copies + ext_c_copies:
@@ -665,7 +664,7 @@
             pltpu.SemaphoreType.DMA((10,)),
             pltpu.SemaphoreType.DMA((33,)),
             pltpu.SemaphoreType.DMA((33,)),
-            pltpu.SemaphoreType.DMA((15,)),
+            pltpu.SemaphoreType.DMA((16,)),
             pltpu.SemaphoreType.DMA((10,)),
             pltpu.SemaphoreType.DMA((N_PIECE,)),
             pltpu.SemaphoreType.DMA((N_PIECE,)),

time: 221 us -> 230 us (1.041)
  Pallas kernels: 217 us -> 225 us
    pallas_call x1, Pallas kernels: 217 us -> 225 us  [shards(): pl.pallas_call(kernel, out_shape=[jax.ShapeDtypeStruct(flat, jnp.bfloat16...]
where the time goes in v4:
time: 230 us; the launch traced here: 229 us
  Pallas kernels  225 us (98%)
  local copies, waits for them, and re-layouts  2.69 us (1%)
    pallas_call x1, Pallas kernels, shards(): pl.pallas_call(kernel, out_shape=[jax.ShapeDtypeStruct(flat, jnp.bfloat16...  225 us

profile of v4, /device:TPU:16, one launch (start us, length us, event | category | flops | bytes accessed | tf_op | source)
XLA Modules:
  0.0 229.4 jit_solution(15398182140655529855)
XLA Ops:
  1.3 225.4 %shard_map.86 = (bf16[2,192,640]{2,1,0:T(8,128)(2,1)}, bf16[2,192,640]{2,1,0:T(8,128)(2,1)}) custom-call(s32[2,5]{1,0:T(2,128)} %bitcast.15, s32[1]{0:T(128)S(6)} %copy.11.step_ref, bf16[2,192,640]{2,1,0:T(8,128)(2,1)} %bitcast.9, bf16[2,192,640]{2,1,0:T(8,128)(2,1)} %bitcast.10, bf16[2,2,192,640]{3,2,1,0:T(8,128)(2,1)} %bitcast.8, ...), custom_call_target="tpu_custom_call" | custom-call | tf_op jit(solution)/shard_map/pallas_call | solution.py:642
  226.7 0.0 copy-start
  226.7 1.9 copy.12
  228.6 0.0 copy-done
  228.6 0.8 copy.13
Async XLA Ops:
  226.7 1.9 copy-start

commit v5 on v2

--- a/solution.py
+++ b/solution.py
@@ -50,6 +50,7 @@
     o_part,
     m_part,
     l_part,
+    w_far,
     slot_r,
     slot_l,
     mixed,
@@ -92,6 +93,15 @@
     is_via = (wa == 4) | (wa == 11)
     is_direct = has_far & (wa != 4) & (wa != 11)
 
+    @pl.when(is_relay)
+    def _():
+        far[...] = jnp.zeros_like(far)
+
+    barrier = pltpu.get_barrier_semaphore()
+    peers = [dev_par, dev_far, dev_z, dev_diag] + dev_x + dev_y + dev_t
+    for peer in peers:
+        pl.semaphore_signal(barrier, inc=1, device_id=peer, device_id_type=MESH)
+
     loads = []
     for f in range(FRAMES):
         for r in range(T_ROWS):
@@ -113,22 +123,6 @@
     load_h.start()
     load_m.start()
 
-    @pl.when(is_relay)
-    def _():
-        far[...] = jnp.zeros_like(far)
-
-    @pl.when(g == 0)
-    def _():
-        slot_r[...] = jnp.zeros_like(slot_r)
-
-    @pl.when(g == N_TA - 1)
-    def _():
-        slot_l[...] = jnp.zeros_like(slot_l)
-
-    barrier = pltpu.get_barrier_semaphore()
-    peers = [dev_par, dev_far, dev_z, dev_diag] + dev_x + dev_y + dev_t
-    for peer in peers:
-        pl.semaphore_signal(barrier, inc=1, device_id=peer, device_id_type=MESH)
     for load in loads:
         load.wait()
     load_w.wait()
@@ -152,15 +146,15 @@
     def far_rows_b(src, device):
         return remote(2, rows(src, 3, 1), rows(far, 3, 1), device)
 
-    def middle(buf, head):
-        return buf.at[:, pl.ds(2 * TOK, TOK), pl.ds(head * HD, HD)]
-
-    def far_head(head, src, device):
-        return remote(28 + head, middle(src, head), middle(far, head), device)
+    def middle(buf, which):
+        return buf.at[which, pl.ds(2 * TOK, TOK), :]
+
+    def far_rows_v(src, device):
+        return remote(28, middle(src, 1), middle(far, 1), device)
 
     far_b = far_rows_b(own, dev_far)
-    far_c = [far_head(head, own, dev_far) for head in range(HEADS_HERE)]
-    passed = range(3, HEADS_HERE)
+    far_k = remote(3, middle(own, 0), middle(far, 0), dev_far)
+    far_v = far_rows_v(own, dev_far)
     up = remote(4, rows(own, 1, 1), rows(own, 4, 1), dev_x[2])
     down = remote(5, rows(own, 3, 1), rows(own, 0, 1), dev_x[0])
     par_mid = remote(6, rows(own, 1, 3), rows(par, 1, 3), dev_par)
@@ -202,8 +196,7 @@
     @pl.when(is_via)
     def _():
         far_rows_b(own, dev_via).start()
-        for head in passed:
-            far_head(head, own, dev_via).start()
+        far_rows_v(own, dev_via).start()
 
     up.start()
     down.start()
@@ -224,6 +217,14 @@
     w_c[1].start()
     for copy in w_yf:
         copy.start()
+
+    @pl.when(g == 0)
+    def _():
+        slot_r[...] = jnp.zeros_like(slot_r)
+
+    @pl.when(g == N_TA - 1)
+    def _():
+        slot_l[...] = jnp.zeros_like(slot_l)
 
     par_mid.wait_recv()
     par_top.wait_recv()
@@ -298,19 +299,12 @@
     @pl.when(has_far)
     def _():
         far_a.wait_send()
-        for head in range(3):
-            far_c[head].start()
-
-    @pl.when(is_direct)
-    def _():
-        for head in passed:
-            far_c[head].start()
+        far_k.start()
 
     @pl.when(is_relay)
     def _():
-        for head in passed:
-            far_c[head].wait_recv()
-            far_head(head, far, dev_diag).start()
+        far_v.wait_recv()
+        far_rows_v(far, dev_diag).start()
 
     @pl.when(has_far)
     def _():
@@ -330,42 +324,51 @@
         w_yf[j].wait_recv()
         w_c[5 + j].start()
 
+    @pl.when(is_direct)
+    def _():
+        far_k.wait_send()
+        far_v.start()
+
     @pl.when(has_far)
     def _():
         far_up.wait_recv()
         far_down.wait_recv()
-
-    def far_tile(r, head):
-        index = r * HEADS_HERE + head
+        far_k.wait_recv()
+
+    def far_weights(index, carry):
+        r = index // HEADS_HERE
+        head = lax.rem(index, HEADS_HERE)
         query = query_tile(r, head)
         s_far = scores(query, far, r, head, biases(r, head, True, far_there))
         before = m_part[index]
-        highest = jnp.maximum(
-            before, jnp.max(total(s_far, jnp.maximum), axis=1, keepdims=True)
-        )
+        highest = jnp.maximum(before, jnp.max(total(s_far, jnp.maximum), axis=1, keepdims=True))
         shrink = jnp.exp(before - highest)
         p_far = [jnp.exp(s - highest) for s in s_far]
         norm = shrink * l_part[index] + jnp.sum(total(p_far, jnp.add), axis=1, keepdims=True)
-        out = (shrink * o_part[index] + values(p_far, far, r, head)) / norm
-        att[token_rows(r, 1), lanes(head)] = out.astype(jnp.bfloat16)
-
-    def far_step(head, carry):
-        @pl.when(has_far)
-        def _():
-            pltpu.make_async_remote_copy(
-                src_ref=middle(own, 0),
-                dst_ref=middle(far, 0),
-                send_sem=ssem.at[28 + head],
-                recv_sem=rsem.at[28 + head],
-                device_id=dev_far,
-                device_id_type=MESH,
-            ).wait_recv()
-
+        share_of = 1.0 / norm
+        o_part[index] = o_part[index] * (shrink * share_of)
+        for j in range(3):
+            w_far[index, :, j * TOK : (j + 1) * TOK] = (p_far[j] * share_of).astype(jnp.bfloat16)
+        return carry
+
+    lax.fori_loop(0, T_ROWS * HEADS_HERE, far_weights, 0)
+
+    @pl.when(has_far)
+    def _():
+        far_v.wait_recv()
+
+    def far_values(head, carry):
         for r in range(T_ROWS):
-            far_tile(r, head)
+            index = r * HEADS_HERE + head
+            out = o_part[index] + jnp.dot(
+                w_far[index],
+                far[1, token_rows(r, 3), lanes(head)],
+                preferred_element_type=jnp.float32,
+            )
+            att[token_rows(r, 1), lanes(head)] = out.astype(jnp.bfloat16)
         return carry
 
-    lax.fori_loop(0, HEADS_HERE, far_step, 0)
+    lax.fori_loop(0, HEADS_HERE, far_values, 0)
     for copy in w_c:
         copy.wait_recv()
 
@@ -484,15 +487,17 @@
         ffn_ref[0, part, :] = out[:HALF]
         ffn_ref[1, part, :] = out[HALF:]
 
-    for copy in [w_z, far_b, up, down, par_mid, par_top, par_bot]:
+    for copy in [w_z, far_b, far_v, up, down, par_mid, par_top, par_bot]:
         copy.wait_send()
-    for head in passed:
-        far_c[head].wait_send()
-
-    @pl.when(has_far)
-    def _():
-        for copy in [far_up, far_down] + far_c[:3]:
-            copy.wait_send()
+
+    @pl.when(has_far)
+    def _():
+        far_up.wait_send()
+        far_down.wait_send()
+
+    @pl.when(is_via)
+    def _():
+        far_k.wait_send()
 
     for copy in w_x + w_yn + w_yf + w_c:
         copy.wait_send()
@@ -538,13 +543,14 @@
             pltpu.VMEM((tiles, TOK, HD), jnp.float32),
             pltpu.VMEM((tiles, TOK, HD), jnp.float32),
             pltpu.VMEM((tiles, TOK, HD), jnp.float32),
+            pltpu.VMEM((tiles, TOK, 3 * TOK), jnp.bfloat16),
             pltpu.VMEM((N_PIECE, TOK, FEAT), jnp.bfloat16),
             pltpu.VMEM((N_PIECE, TOK, FEAT), jnp.bfloat16),
             pltpu.VMEM((TOKENS, FEAT), jnp.float32),
             pltpu.VMEM((N_TA, T_ROWS, 8, HD), jnp.float32),
             pltpu.SemaphoreType.DMA((10,)),
-            pltpu.SemaphoreType.DMA((33,)),
-            pltpu.SemaphoreType.DMA((33,)),
+            pltpu.SemaphoreType.DMA((29,)),
+            pltpu.SemaphoreType.DMA((29,)),
             pltpu.SemaphoreType.DMA((N_PIECE,)),
             pltpu.SemaphoreType.DMA((N_PIECE,)),
             pltpu.SemaphoreType.DMA((N_PIECE,)),
@@ -553,7 +559,7 @@
             pltpu.SemaphoreType.DMA((7 * T_ROWS,)),
         ],
         compiler_params=pltpu.CompilerParams(
-            collective_id=0, has_side_effects=True, vmem_limit_bytes=52 * 2**20
+            collective_id=0, has_side_effects=True, vmem_limit_bytes=60 * 2**20
         ),
     )(
         windows.T,

time: 198 us -> 197 us (level)
  the two profiles are of different devices: /device:TPU:12 before, /device:TPU:10 now
where the time goes in v5:
time: 197 us
  Pallas kernels  193 us (98%)
  local copies, waits for them, and re-layouts  2.69 us (1%)
    pallas_call x1, Pallas kernels, shards(): pl.pallas_call(kernel, out_shape=[jax.ShapeDtypeStruct(flat, jnp.bfloat16...  193 us

profile of v5, /device:TPU:10, one launch (start us, length us, event | category | flops | bytes accessed | tf_op | source)
XLA Modules:
  0.0 197.0 jit_solution(7305407417933083422)
XLA Ops:
  1.3 193.1 %shard_map.86 = (bf16[2,192,640]{2,1,0:T(8,128)(2,1)}, bf16[2,192,640]{2,1,0:T(8,128)(2,1)}) custom-call(s32[2,5]{1,0:T(2,128)} %bitcast.15, s32[1]{0:T(128)S(6)} %copy.11.step_ref, bf16[2,192,640]{2,1,0:T(8,128)(2,1)} %bitcast.9, bf16[2,192,640]{2,1,0:T(8,128)(2,1)} %bitcast.10, bf16[2,2,192,640]{3,2,1,0:T(8,128)(2,1)} %bitcast.8, ...), custom_call_target="tpu_custom_call" | custom-call | tf_op jit(solution)/shard_map/pallas_call | solution.py:529
  194.3 0.0 copy-start
  194.4 1.9 copy.12
  196.3 0.0 copy-done
  196.3 0.8 copy.13
Async XLA Ops:
  194.3 1.9 copy-start

commit v6 on v5

--- a/solution.py
+++ b/solution.py
@@ -252,7 +252,7 @@
         return out
 
     def lanes(head):
-        return pl.ds(pl.multiple_of(head * HD, HD), HD)
+        return pl.ds(head * HD if isinstance(head, int) else pl.multiple_of(head * HD, HD), HD)
 
     def token_rows(r, count):
         return pl.ds(r * TOK if isinstance(r, int) else pl.multiple_of(r * TOK, TOK), count * TOK)
@@ -357,18 +357,6 @@
     def _():
         far_v.wait_recv()
 
-    def far_values(head, carry):
-        for r in range(T_ROWS):
-            index = r * HEADS_HERE + head
-            out = o_part[index] + jnp.dot(
-                w_far[index],
-                far[1, token_rows(r, 3), lanes(head)],
-                preferred_element_type=jnp.float32,
-            )
-            att[token_rows(r, 1), lanes(head)] = out.astype(jnp.bfloat16)
-        return carry
-
-    lax.fori_loop(0, HEADS_HERE, far_values, 0)
     for copy in w_c:
         copy.wait_recv()
 
@@ -402,7 +390,7 @@
         )
 
     def hop(tau, carry):
-        k = tau - 2 * g
+        k = tau - T_ROWS * g
 
         @pl.when((k >= 0) & (k < T_ROWS * (N_TA - 1 - g)))
         def _():
@@ -414,7 +402,7 @@
             slot_r[k] = (slot_r[k].astype(jnp.float32) + add).astype(jnp.bfloat16)
             hop_r(k).start()
 
-        n = tau - 2 * (N_TA - 1 - g)
+        n = tau - T_ROWS * (N_TA - 1 - g)
 
         @pl.when((n >= 0) & (n < T_ROWS * g))
         def _():
@@ -428,7 +416,19 @@
 
         return carry
 
-    lax.fori_loop(0, T_ROWS * (N_TA - 1), hop, 0)
+    def finish_row(r, carry):
+        for head in range(HEADS_HERE):
+            index = r * HEADS_HERE + head
+            out = o_part[index] + jnp.dot(
+                w_far[index],
+                far[1, token_rows(r, 3), lanes(head)],
+                preferred_element_type=jnp.float32,
+            )
+            att[token_rows(r, 1), lanes(head)] = out.astype(jnp.bfloat16)
+        return hop(r, carry)
+
+    lax.fori_loop(0, T_ROWS, finish_row, 0)
+    lax.fori_loop(T_ROWS, T_ROWS * (N_TA - 1), hop, 0)
 
     load_h.wait()
     load_m.wait()

time: 197 us -> 197 us (level)
  no operation moved by 1% of the time
where the time goes in v6:
time: 197 us
  Pallas kernels  193 us (98%)
  local copies, waits for them, and re-layouts  2.69 us (1%)
    pallas_call x1, Pallas kernels, shards(): pl.pallas_call(kernel, out_shape=[jax.ShapeDtypeStruct(flat, jnp.bfloat16...  193 us

profile of v6, /device:TPU:10, one launch (start us, length us, event | category | flops | bytes accessed | tf_op | source)
XLA Modules:
  0.0 197.0 jit_solution(6871597358987866320)
XLA Ops:
  1.3 193.1 %shard_map.86 = (bf16[2,192,640]{2,1,0:T(8,128)(2,1)}, bf16[2,192,640]{2,1,0:T(8,128)(2,1)}) custom-call(s32[2,5]{1,0:T(2,128)} %bitcast.15, s32[1]{0:T(128)S(6)} %copy.11.step_ref, bf16[2,192,640]{2,1,0:T(8,128)(2,1)} %bitcast.9, bf16[2,192,640]{2,1,0:T(8,128)(2,1)} %bitcast.10, bf16[2,2,192,640]{3,2,1,0:T(8,128)(2,1)} %bitcast.8, ...), custom_call_target="tpu_custom_call" | custom-call | tf_op jit(solution)/shard_map/pallas_call | solution.py:529
  194.3 0.0 copy-start
  194.4 1.9 copy.12
  196.3 0.0 copy-done
  196.3 0.8 copy.13
Async XLA Ops:
  194.3 1.9 copy-start

commit v7 on v6

--- a/solution.py
+++ b/solution.py
@@ -320,14 +320,14 @@
         far_b.wait_recv()
         far_down.start()
 
+    @pl.when(is_direct)
+    def _():
+        far_k.wait_send()
+        far_v.start()
+
     for j in range(3):
         w_yf[j].wait_recv()
         w_c[5 + j].start()
-
-    @pl.when(is_direct)
-    def _():
-        far_k.wait_send()
-        far_v.start()
 
     @pl.when(has_far)
     def _():

time: 197 us -> 197 us (level)
  no operation moved by 1% of the time
where the time goes in v7:
time: 197 us
  Pallas kernels  193 us (98%)
  local copies, waits for them, and re-layouts  2.69 us (1%)
    pallas_call x1, Pallas kernels, shards(): pl.pallas_call(kernel, out_shape=[jax.ShapeDtypeStruct(flat, jnp.bfloat16...  193 us

profile of v7, /device:TPU:10, one launch (start us, length us, event | category | flops | bytes accessed | tf_op | source)
XLA Modules:
  0.0 197.0 jit_solution(7036709415264777721)
XLA Ops:
  1.3 193.1 %shard_map.86 = (bf16[2,192,640]{2,1,0:T(8,128)(2,1)}, bf16[2,192,640]{2,1,0:T(8,128)(2,1)}) custom-call(s32[2,5]{1,0:T(2,128)} %bitcast.15, s32[1]{0:T(128)S(6)} %copy.11.step_ref, bf16[2,192,640]{2,1,0:T(8,128)(2,1)} %bitcast.9, bf16[2,192,640]{2,1,0:T(8,128)(2,1)} %bitcast.10, bf16[2,2,192,640]{3,2,1,0:T(8,128)(2,1)} %bitcast.8, ...), custom_call_target="tpu_custom_call" | custom-call | tf_op jit(solution)/shard_map/pallas_call | solution.py:529
  194.3 0.0 copy-start
  194.4 1.9 copy.12
  196.3 0.0 copy-done
  196.3 0.8 copy.13
Async XLA Ops:
  194.3 1.9 copy-start
